TPU v7x, 32 devices: a whole 2x2x4 slice. The times are simulated.
32 devices in a mesh: replica: 4 (over y, x), fsdp: 8 (over z, core).
Axes of the slice: x: 2, y: 2, z: 4, core: 2. Of those that a mesh axis runs over, the one named last changes fastest.
Arguments:
- anchor: float32 [3328, 3328], P('fsdp', 'replica'), may hold values from -6 to 6
- prev_delta: bfloat16 [4, 3328, 3328], P('replica', 'fsdp'), may hold values from -4 to 4
- momentum: float32 [3328, 3328], P('fsdp', 'replica'), may hold values from -2 to 2
- pool: bfloat16 [4, 256, 3328], P('replica', 'fsdp'), may hold values from -6 to 6
- ids: int32 [4, 2, 256], P('replica', None, 'fsdp'), may hold values from 0 to 31
- cotangent: bfloat16 [4, 2, 3328, 256], P('replica', None, 'fsdp'), may hold values from -6 to 6
Outputs:
- new_delta: bfloat16 [4, 3328, 3328], P('replica', 'fsdp')
- new_anchor: float32 [3328, 3328], P('fsdp', 'replica')
- new_momentum: float32 [3328, 3328], P('fsdp', 'replica')
All inputs are finite; a program needn't handle non-finite values.
Results may differ from a plain program's by a relative error of at most 0.0062.
Values may be sent and summed in bfloat16 or wider, within the bound.
A program may use at most 64 MiB of HBM per device.

v0:
```python
import math

import jax
import jax.numpy as jnp
from jax import lax
from jax.sharding import PartitionSpec as P

D = 3328
HW = 3328


INNER_RATE = 2.0
INNER_DECAY = 0.1
PENALTY = 0.5
MOMENT_DECAY = 0.9
OUTER_RATE = 0.7
CLIP_SHARE = 0.05


def silu_slope(preact):
    sigmoid_val = jax.nn.sigmoid(preact)
    return sigmoid_val * (1.0 + preact * (1.0 - sigmoid_val))


def row_gradient(portion, rounded, cot_step, root_width):
    preact = (
        lax.dot_general(
            rounded, portion, (((1,), (1,)), ((), ())), preferred_element_type=jnp.float32
        )
        / root_width
    )
    scaled = (cot_step.astype(jnp.float32) * silu_slope(preact)).astype(jnp.bfloat16)
    return jnp.dot(scaled, portion, preferred_element_type=jnp.float32)


def island_mean(prev_delta):
    summed = lax.psum_scatter(
        prev_delta[0].astype(jnp.float32).astype(jnp.bfloat16),
        "replica",
        scatter_dimension=1,
        tiled=True,
    ).astype(jnp.float32)
    return summed / lax.axis_size("replica")


def body(anchor, prev_delta, momentum, pool, ids, cotangent):
    root_width = math.sqrt(D)
    anchor_island = lax.all_gather(anchor, "replica", axis=1, tiled=True)
    own_rows = jnp.take(pool[0], ids[0], axis=0)
    weights = anchor_island
    zero_grad = jnp.zeros(anchor_island.shape, jnp.float32)
    for inner_step in range(ids.shape[1]):
        rounded = weights.astype(jnp.bfloat16)
        cot_step = cotangent[0, inner_step]

        def accumulate(running, portion, first, rounded=rounded, cot_step=cot_step):
            return row_gradient(portion, rounded, cot_step, root_width)

        gradient = accumulate(
            zero_grad,
            lax.all_gather(own_rows[inner_step], "fsdp", axis=0, tiled=True),
            jnp.int32(0),
        )
        weights = weights - INNER_RATE * (gradient / root_width) - INNER_DECAY * weights
    new_delta = (anchor_island - weights).astype(jnp.bfloat16)[None]
    averaged = island_mean(prev_delta)
    corrected = averaged + PENALTY * (averaged - momentum)
    squares = lax.psum(jnp.sum(corrected * corrected), ("replica", "fsdp"))
    max_norm = CLIP_SHARE * math.sqrt(D * HW)
    factor = jnp.minimum(1.0, max_norm / jnp.sqrt(squares + 1e-06))
    clipped = factor * corrected
    new_momentum = MOMENT_DECAY * momentum + clipped
    new_anchor = anchor - OUTER_RATE * (MOMENT_DECAY * new_momentum + clipped)
    return (new_delta, new_anchor, new_momentum)


def solution(mesh):
    return jax.shard_map(
        body,
        mesh=mesh,
        in_specs=(
            P("fsdp", "replica"),
            P("replica", "fsdp", None),
            P("fsdp", "replica"),
            P("replica", "fsdp", None),
            P("replica", None, "fsdp"),
            P("replica", None, "fsdp", None),
        ),
        out_specs=(P("replica", "fsdp", None), P("fsdp", "replica"), P("fsdp", "replica")),
        check_vma=False,
    )
```

profile of v0, /device:TPU:0, one launch (start us, length us, event | category | flops | bytes accessed | tf_op | source)
XLA Modules:
  0.0 204.7 jit_solution(14482791961008062487)
XLA Ops:
  7.2 0.0 copy-start
  7.2 0.0 reduce-scatter.4.cloned.1.call-start
  7.2 5.4 %copy.11 = bf16[416,3328]{0,1:T(8,128)(2,1)} copy(bf16[416,3328]{1,0:T(8,128)(2,1)} %bitcast.81) | data formatting | bytes 5537792
  12.6 0.0 copy-start.3
  12.6 0.0 reduce-scatter.4.cloned.1.call-update
  12.7 0.0 all-gather.11.cloned.1.call-start
  12.7 0.7 all-gather.11.cloned.1.call-update
  13.4 0.0 all-gather.7.cloned.1.call-start
  13.5 0.0 copy-done.3
  13.5 0.1 reshape.48
  13.6 0.0 copy-done
  13.6 0.8 gather_fusion
  14.4 0.0 copy-start.1
  14.4 0.1 broadcast_select_fusion
  14.5 0.8 fusion.52
  15.3 0.0 all-gather.7.cloned.1.call-update
  15.3 0.0 all-gather.9.cloned.1.call-start
  15.4 0.5 all-gather.9.cloned.1.call-update
  15.9 45.7 %reduce-scatter.4.cloned.1.call-done = bf16[832,416]{1,0:T(8,128)(2,1)} async-done(((bf16[3328,416]{1,0:T(8,128)(2,1)}), bf16[832,416]{1,0:T(8,128)(2,1)}) %reduce-scatter.4.cloned.1.call-update) | async-done | bytes 692240
  61.7 1.8 copy.12
  63.4 0.0 copy-done.1
  63.5 1.0 multiply_reduce_fusion
  64.5 39.8 %psum.7 = f32[]{:T(128)} all-reduce(f32[]{:T(128)} %multiply_reduce_fusion), channel_id=1, replica_groups=mesh['replica'=4,'fsdp'=8] {'replica','fsdp'}, use_global_device_ids=true, to_apply=%region_2.3 | all-reduce | flops 1 | bytes 8 | tf_op jit(solution)/shard_map/psum | solution.py:68
  105.0 3.6 %multiply_subtract_fusion = (f32[416,832]{1,0:T(8,128)}, f32[416,832]{1,0:T(8,128)}) fusion(f32[416,832]{1,0:T(8,128)} %param.6, f32[416,832]{1,0:T(8,128)S(1)} %copy-done.1, bf16[416,832]{1,0:T(8,128)(2,1)S(1)} %copy.12, f32[]{:T(128)S(6)} %min.3), kind=kLoop, calls=%fused_computation.19 | loop fusion | flops 4153344 | bytes 6230020 | tf_op jit(solution)/shard_map/sub | solution.py:73
  108.6 23.1 %all-gather.11.cloned.1.call-done = f32[4,832,416]{1,2,0:T(8,128)} async-done(((f32[1,832,416]{1,2,0:T(8,128)}), f32[4,832,416]{1,2,0:T(8,128)}) %all-gather.11.cloned.1.call-update) | async-done | bytes 5537808 | tf_op jit(solution)/shard_map/all_gather | solution.py:48
  131.7 9.1 %copy.10 = f32[4,832,416]{1,0,2:T(4,128)} copy(f32[4,832,416]{1,2,0:T(8,128)} %all-gather.11.cloned.1.call-done) | data formatting | bytes 11075584 | tf_op jit(solution)/shard_map/all_gather | solution.py:48
  140.8 0.0 copy-start.2
  140.8 8.1 %reshape.58 = f32[3328,416]{0,1:T(8,128)} reshape(f32[4,832,416]{1,0,2:T(4,128)} %copy.10) | data formatting | bytes 11075584
  148.9 10.4 %all-gather.7.cloned.1.call-done = bf16[1,256,3328]{2,1,0:T(8,128)(2,1)} async-done(((bf16[1,32,3328]{2,1,0:T(8,128)(2,1)}), bf16[1,256,3328]{2,1,0:T(8,128)(2,1)}) %all-gather.7.cloned.1.call-update) | async-done | bytes 1703952 | tf_op jit(solution)/shard_map/all_gather | solution.py:61
  159.3 0.0 copy-done.2
  159.3 10.8 %fusion.3 = f32[416,3328]{1,0:T(8,128)} fusion(f32[3328,416]{0,1:T(8,128)} %reshape.58, bf16[1,256,3328]{2,1,0:T(8,128)(2,1)} %all-gather.7.cloned.1.call-done, bf16[1,2,416,256]{3,2,1,0:T(8,128)(2,1)S(1)} %copy-done.2), kind=kOutput, calls=%fused_computation.6 | convolution fusion | flops 1424384000 | bytes 20234240 | tf_op jit(solution)/shard_map/dot_general | solution.py:33
  170.1 16.7 %all-gather.9.cloned.1.call-done = bf16[1,256,3328]{2,1,0:T(8,128)(2,1)} async-done(((bf16[1,32,3328]{2,1,0:T(8,128)(2,1)}), bf16[1,256,3328]{2,1,0:T(8,128)(2,1)}) %all-gather.9.cloned.1.call-update) | async-done | bytes 1703952 | tf_op jit(solution)/shard_map/all_gather | solution.py:61
  186.8 11.4 %fusion.6 = bf16[1,416,3328]{2,1,0:T(8,128)(2,1)} fusion(f32[416,3328]{1,0:T(8,128)} %fusion.3, f32[3328,416]{0,1:T(8,128)} %reshape.58, bf16[1,256,3328]{2,1,0:T(8,128)(2,1)} %all-gather.9.cloned.1.call-done, bf16[1,2,416,256]{3,2,1,0:T(8,128)(2,1)S(1)} %copy-done.2), kind=kOutput, calls=%fused_computation.11 | convolution fusion | flops 1428537344 | bytes 23003136 | tf_op jit(solution)/shard_map/dot_general | solution.py:33
  (3 shorter events, 0.0 us)
Async XLA Ops:
  7.2 6.4 %copy-start = (bf16[1,32,3328]{2,1,0:T(8,128)(2,1)S(1)}, bf16[1,32,3328]{2,1,0:T(8,128)(2,1)}, u32[]{:S(2)}) copy-start(bf16[1,32,3328]{2,1,0:T(8,128)(2,1)} %param.9) | copy-start | bytes 638980
  7.2 54.5 %reduce-scatter.4.cloned.1.call-start = ((), (), s32[]{:S(2)}) async-start(), calls=%async_computation.4 | async-start | bytes 4259840
  12.6 0.8 copy-start.3
  12.7 119.1 %all-gather.11.cloned.1.call-start = ((), (), s32[]{:S(2)}) async-start(), calls=%async_computation.3 | async-start | bytes 7454720 | tf_op jit(solution)/shard_map/all_gather | solution.py:48
  13.4 145.9 %all-gather.7.cloned.1.call-start = ((), (), s32[]{:S(2)}) async-start(), calls=%async_computation.1 | async-start | bytes 1916928 | tf_op jit(solution)/shard_map/all_gather | solution.py:61
  14.4 49.0 %copy-start.1 = (f32[416,832]{1,0:T(8,128)S(1)}, f32[416,832]{1,0:T(8,128)}, u32[]{:S(2)}) copy-start(f32[416,832]{1,0:T(8,128)} %param.8) | copy-start | bytes 4153348
  15.3 171.4 %all-gather.9.cloned.1.call-start = ((), (), s32[]{:S(2)}) async-start(), calls=%async_computation.2 | async-start | bytes 1916928 | tf_op jit(solution)/shard_map/all_gather | solution.py:61
  140.8 18.4 %copy-start.2 = (bf16[1,2,416,256]{3,2,1,0:T(8,128)(2,1)S(1)}, bf16[1,2,416,256]{3,2,1,0:T(8,128)(2,1)}, u32[]{:S(2)}) copy-start(bf16[1,2,416,256]{3,2,1,0:T(8,128)(2,1)} %param.11) | copy-start | bytes 1277956
Sparse Core Ops, SparseCore 0:
  12.8 48.8 reduce-scatter.3
  63.5 68.1 all-gather.10
  133.4 25.8 all-gather.6
  161.4 25.3 all-gather.8
where the time goes:
time: 205 us
  waiting for transfers between devices  97.2 us (47%)
  blocking collectives  39.8 us (19%)
  local copies, waits for them, and re-layouts  26.1 us (13%)
  matrix products  22.2 us (11%)
  between operations  14.5 us (7%)
  other arithmetic  4.72 us (2%)
    unnamed x5, waiting for transfers between devices  47 us
    psum x1, blocking collectives, body(): squares = lax.psum(jnp.sum(corrected * corrected), ('replica', 'fsdp'))  39.8 us
    all_gather x2, waiting for transfers between devices, body(): lax.all_gather(own_rows[inner_step], 'fsdp', axis=0, tiled=True)  27.1 us
    all_gather x1, waiting for transfers between devices, body(): anchor_island = lax.all_gather(anchor, 'replica', axis=1, tiled=True)  23.1 us
    dot_general x2, matrix products, row_gradient(): return jnp.dot(scaled, portion, preferred_element_type=jnp.float32)  22.2 us
    unnamed x11, local copies, waits for them, and re-layouts  15.3 us
    all_gather x1, local copies, waits for them, and re-layouts, body(): anchor_island = lax.all_gather(anchor, 'replica', axis=1, tiled=True)  9.1 us
  transfers between devices with their start and end apart: 4, of which 4 were waited for; matrix products, arithmetic and copies ran while one was open for 18% of the time, Pallas kernels for 0%

commit v1 on v0

--- a/solution.py
+++ b/solution.py
@@ -1,8 +1,11 @@
+import functools
 import math
 
 import jax
 import jax.numpy as jnp
 from jax import lax
+from jax.experimental import pallas as pl
+from jax.experimental.pallas import tpu as pltpu
 from jax.sharding import PartitionSpec as P
 
 D = 3328
@@ -43,7 +46,7 @@
     return summed / lax.axis_size("replica")
 
 
-def body(anchor, prev_delta, momentum, pool, ids, cotangent):
+def plain_body(anchor, prev_delta, momentum, pool, ids, cotangent):
     root_width = math.sqrt(D)
     anchor_island = lax.all_gather(anchor, "replica", axis=1, tiled=True)
     own_rows = jnp.take(pool[0], ids[0], axis=0)
@@ -74,6 +77,372 @@
     return (new_delta, new_anchor, new_momentum)
 
 
+def contract_last(left, right):
+    return lax.dot_general(
+        left, right, (((1,), (1,)), ((), ())), preferred_element_type=jnp.float32
+    )
+
+
+def exchange_kernel(
+    n_fsdp,
+    ids_ref, prev_ref, anchor_ref, mom_ref, pool_ref, cot_ref,
+    ag_out, bb_out, corr_out, scaled_out, sq_out,
+    pv, blk, av, mv, plv, cv, ag, poolb, selb, bb, xr, yr, qs, s2, corr, preact, gram, sqv,
+    local_sem, out_sem, send_sem, recv_sem, pool_send, pool_recv, sel_send, sel_recv,
+):
+    r = lax.axis_index("replica")
+    f = lax.axis_index("fsdp")
+    rx = r + 1 - 2 * (r % 2)
+    ry = r + 2 - 4 * (r // 2)
+    rd = 3 - r
+    fs = f + 1 - 2 * (f % 2)
+    hops = list(range(1, n_fsdp // 2))
+    x_dev, y_dev, sib_dev = (rx, f), (ry, f), (r, fs)
+    z_to = {k: (r, (f + 2 * k) % n_fsdp) for k in hops}
+    rows, width = anchor_ref.shape
+    half = rows // 2
+    tok = poolb.shape[2]
+    n_tok = n_fsdp * tok
+    root_width = math.sqrt(pv.shape[1])
+    lower, upper = pl.ds(0, half), pl.ds(half, half)
+
+    def local(src, dst, index):
+        copy = pltpu.make_async_copy(src, dst, local_sem.at[index])
+        copy.start()
+        return copy
+
+    def remote(src, dst, index, dev, sends=send_sem, recvs=recv_sem):
+        return pltpu.make_async_remote_copy(
+            src_ref=src,
+            dst_ref=dst,
+            send_sem=sends.at[index],
+            recv_sem=recvs.at[index],
+            device_id=dev,
+            device_id_type=pl.DeviceIdType.MESH,
+        )
+
+    in_pool = local(pool_ref.at[0], plv, 0)
+    in_low = local(prev_ref.at[0, lower], pv.at[lower], 1)
+    in_up = local(prev_ref.at[0, upper], pv.at[upper], 2)
+    in_anchor = local(anchor_ref, av, 3)
+    in_mom = local(mom_ref, mv, 4)
+    in_cot = local(cot_ref.at[0], cv, 5)
+
+    barrier = pltpu.get_barrier_semaphore()
+    partners = [x_dev, y_dev, sib_dev] + [z_to[k] for k in hops]
+    for dev in partners:
+        pl.semaphore_signal(barrier, inc=1, device_id=dev, device_id_type=pl.DeviceIdType.MESH)
+
+    in_low.wait()
+    for j in range(4):
+        blk[j, lower, :] = pv[lower, width * j : width * (j + 1)]
+    pl.semaphore_wait(barrier, len(partners))
+    started = []
+
+    def send(src, dst, index, dev):
+        copy = remote(src, dst, index, dev)
+        copy.start()
+        started.append(copy)
+        return copy
+
+    rs_xd = send(blk.at[rd, lower], xr.at[0], 0, x_dev)
+    rs_xo = send(blk.at[rx, lower], xr.at[1], 1, x_dev)
+    in_up.wait()
+    for j in range(4):
+        blk[j, upper, :] = pv[upper, width * j : width * (j + 1)]
+    rs_yd = send(blk.at[rd, upper], yr.at[0], 2, y_dev)
+    rs_yo = send(blk.at[ry, upper], yr.at[1], 3, y_dev)
+
+    in_pool.wait()
+    for j in range(4):
+        poolb[f, j] = plv[:, width * j : width * (j + 1)]
+    square = (tok, tok)
+    eye = lax.broadcasted_iota(jnp.int32, square, 0) == lax.broadcasted_iota(jnp.int32, square, 1)
+    lane = lax.broadcasted_iota(jnp.int32, (tok, n_tok), 1).astype(jnp.float32)
+    base = (f * tok).astype(jnp.float32)
+    for k in range(2):
+        chosen = jnp.broadcast_to(ids_ref[0, k : k + 1, :].astype(jnp.float32), square)
+        column = jnp.sum(jnp.where(eye, chosen, 0.0), axis=1, keepdims=True)
+        selb[f, k] = jnp.where(lane == column + base, 1.0, 0.0).astype(jnp.bfloat16)
+
+    pool_moves = []
+
+    def pool_move(slot, index, dev):
+        for buf, sends, recvs in ((poolb, pool_send, pool_recv), (selb, sel_send, sel_recv)):
+            copy = remote(buf.at[slot], buf.at[slot], index, dev, sends, recvs)
+            copy.start()
+            pool_moves.append(copy)
+
+    def pool_arrival(slot, index, dev):
+        for buf, sends, recvs in ((poolb, pool_send, pool_recv), (selb, sel_send, sel_recv)):
+            remote(buf.at[slot], buf.at[slot], index, dev, sends, recvs).wait_recv()
+
+    for k in hops:
+        pool_move(f, k, z_to[k])
+    n_line = n_fsdp // 2
+    pool_move(f, n_line, sib_dev)
+
+    in_anchor.wait()
+    ag[r] = av[...].astype(jnp.bfloat16)
+    send(ag.at[r, lower], ag.at[r, lower], 6, x_dev)
+    send(ag.at[r, upper], ag.at[r, upper], 7, y_dev)
+
+    rs_xd.wait_recv()
+    qs[0] = (blk[ry, lower, :].astype(jnp.float32) + xr[0].astype(jnp.float32)).astype(jnp.bfloat16)
+    s2_y = send(qs.at[0], s2.at[0], 4, y_dev)
+    rs_yd.wait_recv()
+    qs[1] = (blk[rx, upper, :].astype(jnp.float32) + yr[0].astype(jnp.float32)).astype(jnp.bfloat16)
+    s2_x = send(qs.at[1], s2.at[1], 5, x_dev)
+    send(ag.at[r, upper], ag.at[r, upper], 8, x_dev)
+    send(ag.at[r, lower], ag.at[r, lower], 9, y_dev)
+
+    remote(ag.at[rx, lower], ag.at[rx, lower], 6, x_dev).wait_recv()
+    send(ag.at[rx, lower], ag.at[rx, lower], 10, y_dev)
+    remote(ag.at[ry, upper], ag.at[ry, upper], 7, y_dev).wait_recv()
+    send(ag.at[ry, upper], ag.at[ry, upper], 11, x_dev)
+
+    for k in hops:
+        slot = (f + n_fsdp - 2 * k) % n_fsdp
+        pool_arrival(slot, k, z_to[k])
+        pool_move(slot, n_line + k, sib_dev)
+
+    rs_xo.wait_recv()
+    rs_yo.wait_recv()
+    in_mom.wait()
+    squares = jnp.zeros((), jnp.float32)
+    for part, first, second, final in ((lower, xr, 0, s2_y), (upper, yr, 1, s2_x)):
+        final.wait_recv()
+        total = blk[r, part, :].astype(jnp.float32) + first[1].astype(jnp.float32)
+        averaged = (total + s2[second].astype(jnp.float32)) / 4.0
+        value = averaged + PENALTY * (averaged - mv[part, :])
+        corr[part, :] = value
+        squares = squares + jnp.sum(value * value)
+    sqv[0] = jnp.full(sqv.shape[1:], squares, jnp.float32)
+    outs = []
+
+    def put(src, dst, index):
+        copy = pltpu.make_async_copy(src, dst, out_sem.at[index])
+        copy.start()
+        outs.append(copy)
+
+    put(corr, corr_out, 0)
+    put(ag.at[r], ag_out.at[r], 1)
+
+    sq_x = send(sqv.at[0], sqv.at[4], 12, x_dev)
+
+    pool_arrival(fs, n_line, sib_dev)
+    for k in hops:
+        pool_arrival((fs + n_fsdp - 2 * k) % n_fsdp, n_line + k, sib_dev)
+
+    @pl.loop(0, 4)
+    def _(j):
+        block = poolb[:, j, :, :].reshape(n_tok, width)
+        for k in range(2):
+            choice = selb[:, k, :, :].reshape(n_tok, n_tok)
+            bb[j, pl.ds(k * n_tok, n_tok), :] = jnp.dot(
+                choice, block, preferred_element_type=jnp.float32
+            ).astype(jnp.bfloat16)
+
+    put(bb, bb_out, 2)
+
+    sq_x.wait_recv()
+    sqv[1] = sqv[0] + sqv[4]
+    sq_y = send(sqv.at[1], sqv.at[5], 13, y_dev)
+
+    gram[...] = jnp.zeros_like(gram)
+
+    @pl.loop(0, 4)
+    def _(j):
+        gram[...] += contract_last(bb[j, pl.ds(0, n_tok), :], bb[j, pl.ds(n_tok, n_tok), :])
+
+    sq_y.wait_recv()
+    sqv[2] = sqv[1] + sqv[5]
+    sq_s = send(sqv.at[2], sqv.at[6], 14, sib_dev)
+
+    def add_preact(j, fresh):
+        @pl.loop(0, 2)
+        def _(h):
+            part = pl.ds(pl.multiple_of(h * half, half), half)
+            value = contract_last(ag[j, part, :], bb[j])
+            preact[part, :] = value if fresh else preact[part, :] + value
+
+    add_preact(r, True)
+
+    sq_s.wait_recv()
+    sqv[3] = sqv[2] + sqv[6]
+    sq_z = [send(sqv.at[3], sqv.at[6 + k], 14 + k, z_to[k]) for k in hops]
+
+    remote(ag.at[rx, upper], ag.at[rx, upper], 8, x_dev).wait_recv()
+    put(ag.at[rx], ag_out.at[rx], 3)
+    add_preact(rx, False)
+    remote(ag.at[ry, lower], ag.at[ry, lower], 9, y_dev).wait_recv()
+    put(ag.at[ry], ag_out.at[ry], 4)
+    add_preact(ry, False)
+
+    whole = sqv[3]
+    for k, copy in zip(hops, sq_z):
+        copy.wait_recv()
+        whole = whole + sqv[6 + k]
+    sq_out[...] = whole
+
+    in_cot.wait()
+    gram_high = gram[...].astype(jnp.bfloat16)
+    gram_low = (gram[...] - gram_high.astype(jnp.float32)).astype(jnp.bfloat16)
+
+    remote(ag.at[rd, lower], ag.at[rd, lower], 10, y_dev).wait_recv()
+    remote(ag.at[rd, upper], ag.at[rd, upper], 11, x_dev).wait_recv()
+    put(ag.at[rd], ag_out.at[rd], 5)
+    add_preact(rd, False)
+
+    @pl.loop(0, 2)
+    def _(h):
+        part = pl.ds(pl.multiple_of(h * half, half), half)
+        first = preact[part, pl.ds(0, n_tok)] / root_width
+        scaled = (cv[0, part, :].astype(jnp.float32) * silu_slope(first)).astype(jnp.bfloat16)
+        scaled_out[part, pl.ds(0, n_tok)] = scaled
+        moved = jnp.dot(scaled, gram_high, preferred_element_type=jnp.float32)
+        moved = moved + jnp.dot(scaled, gram_low, preferred_element_type=jnp.float32)
+        second = (1.0 - INNER_DECAY) * preact[part, pl.ds(n_tok, n_tok)]
+        second = (second - INNER_RATE * (moved / root_width)) / root_width
+        scaled_out[part, pl.ds(n_tok, n_tok)] = (
+            cv[1, part, :].astype(jnp.float32) * silu_slope(second)
+        ).astype(jnp.bfloat16)
+
+    for copy in started:
+        copy.wait_send()
+    for copy in pool_moves:
+        copy.wait_send()
+    for copy in outs:
+        copy.wait()
+
+
+def update_kernel(
+    max_norm, root_width,
+    ag_ref, bb_ref, scaled_ref, sq_ref, corr_ref, mom_ref, anchor_ref,
+    delta_ref, new_anchor_ref, new_mom_ref,
+):
+    width = ag_ref.shape[2]
+    n_tok = bb_ref.shape[1] // 2
+    keep = 1.0 - INNER_DECAY
+    for b in range(2):
+        first = jnp.dot(
+            scaled_ref[:, :n_tok], bb_ref[b, :n_tok, :], preferred_element_type=jnp.float32
+        )
+        second = jnp.dot(
+            scaled_ref[:, n_tok:], bb_ref[b, n_tok:, :], preferred_element_type=jnp.float32
+        )
+        moved = (INNER_RATE * keep / root_width) * first + (INNER_RATE / root_width) * second
+        value = (1.0 - keep * keep) * ag_ref[b].astype(jnp.float32) + moved
+        delta_ref[0, :, width * b : width * (b + 1)] = value.astype(jnp.bfloat16)
+    factor = jnp.minimum(1.0, max_norm / jnp.sqrt(sq_ref[0:1, 0:1] + 1e-06))
+    clipped = factor * corr_ref[...]
+    new_mom = MOMENT_DECAY * mom_ref[...] + clipped
+    new_mom_ref[...] = new_mom
+    new_anchor_ref[...] = anchor_ref[...] - OUTER_RATE * (MOMENT_DECAY * new_mom + clipped)
+
+
+def fast_body(anchor, prev_delta, momentum, pool, ids, cotangent):
+    n_fsdp = lax.axis_size("fsdp")
+    rows, width = anchor.shape
+    full = prev_delta.shape[2]
+    tok = pool.shape[1]
+    n_tok = tok * n_fsdp
+    half = rows // 2
+    n_line = n_fsdp // 2
+    bf16, f32 = jnp.bfloat16, jnp.float32
+    any_spec = pl.BlockSpec(memory_space=pl.ANY)
+    vmem_spec = pl.BlockSpec(memory_space=pltpu.VMEM)
+    dma = pltpu.SemaphoreType.DMA
+    ag, bb, corr, scaled, sq = pl.pallas_call(
+        functools.partial(exchange_kernel, n_fsdp),
+        out_shape=(
+            jax.ShapeDtypeStruct((4, rows, width), bf16),
+            jax.ShapeDtypeStruct((4, 2 * n_tok, width), bf16),
+            jax.ShapeDtypeStruct((rows, width), f32),
+            jax.ShapeDtypeStruct((rows, 2 * n_tok), bf16),
+            jax.ShapeDtypeStruct((8, 128), f32),
+        ),
+        in_specs=[vmem_spec] + [any_spec] * 5,
+        out_specs=(any_spec, any_spec, any_spec, vmem_spec, vmem_spec),
+        scratch_shapes=[
+            pltpu.VMEM((rows, full), bf16),
+            pltpu.VMEM((4, rows, width), bf16),
+            pltpu.VMEM((rows, width), f32),
+            pltpu.VMEM((rows, width), f32),
+            pltpu.VMEM((tok, full), bf16),
+            pltpu.VMEM((2, rows, n_tok), bf16),
+            pltpu.VMEM((4, rows, width), bf16),
+            pltpu.VMEM((n_fsdp, 4, tok, width), bf16),
+            pltpu.VMEM((n_fsdp, 2, tok, n_tok), bf16),
+            pltpu.VMEM((4, 2 * n_tok, width), bf16),
+            pltpu.VMEM((2, half, width), bf16),
+            pltpu.VMEM((2, half, width), bf16),
+            pltpu.VMEM((2, half, width), bf16),
+            pltpu.VMEM((2, half, width), bf16),
+            pltpu.VMEM((rows, width), f32),
+            pltpu.VMEM((rows, 2 * n_tok), f32),
+            pltpu.VMEM((n_tok, n_tok), f32),
+            pltpu.VMEM((6 + n_line, 8, 128), f32),
+            dma((6,)),
+            dma((6,)),
+            dma((14 + n_line,)),
+            dma((14 + n_line,)),
+            dma((2 * n_line,)),
+            dma((2 * n_line,)),
+            dma((2 * n_line,)),
+            dma((2 * n_line,)),
+        ],
+        compiler_params=pltpu.CompilerParams(
+            collective_id=0, has_side_effects=True, vmem_limit_bytes=48 * 1024 * 1024
+        ),
+        name="exchange",
+    )(ids, prev_delta, anchor, momentum, pool, cotangent)
+    quarter = rows // 4
+    by_rows = pl.BlockSpec((quarter, width), lambda c, i: (2 * c + i, 0))
+    delta, new_anchor, new_momentum = pl.pallas_call(
+        functools.partial(update_kernel, CLIP_SHARE * math.sqrt(D * HW), math.sqrt(D)),
+        grid=(2, 2),
+        out_shape=(
+            jax.ShapeDtypeStruct(prev_delta.shape, bf16),
+            jax.ShapeDtypeStruct(anchor.shape, f32),
+            jax.ShapeDtypeStruct(anchor.shape, f32),
+        ),
+        in_specs=[
+            pl.BlockSpec((2, half, width), lambda c, i: (c, i, 0)),
+            pl.BlockSpec((2, 2 * n_tok, width), lambda c, i: (c, 0, 0)),
+            pl.BlockSpec((half, 2 * n_tok), lambda c, i: (i, 0)),
+            pl.BlockSpec((8, 128), lambda c, i: (0, 0)),
+            by_rows,
+            by_rows,
+            by_rows,
+        ],
+        out_specs=(
+            pl.BlockSpec((1, half, 2 * width), lambda c, i: (0, i, c)),
+            by_rows,
+            by_rows,
+        ),
+        compiler_params=pltpu.CompilerParams(vmem_limit_bytes=48 * 1024 * 1024),
+        name="update",
+    )(ag, bb, scaled, sq, corr, momentum, anchor)
+    return (delta, new_anchor, new_momentum)
+
+
+def body(anchor, prev_delta, momentum, pool, ids, cotangent):
+    rows, width = anchor.shape
+    fits = (
+        lax.axis_size("replica") == 4
+        and lax.axis_size("fsdp") % 2 == 0
+        and rows % 32 == 0
+        and width % 64 == 0
+        and pool.shape[1] % 16 == 0
+        and ids.shape[1] == 2
+        and ids.shape[2] == pool.shape[1]
+        and (ids.shape[2] * lax.axis_size("fsdp")) % 128 == 0
+    )
+    chosen = fast_body if fits else plain_body
+    return chosen(anchor, prev_delta, momentum, pool, ids, cotangent)
+
+
 def solution(mesh):
     return jax.shard_map(
         body,

time: 205 us -> 79.9 us (0.39)
  waiting for transfers between devices: 97.2 us -> 0 us
  Pallas kernels: 0 us -> 73.6 us
  blocking collectives: 39.8 us -> 0 us
  matrix products: 22.2 us -> 0 us
  local copies, waits for them, and re-layouts: 26.1 us -> 5.38 us
  between operations: 14.5 us -> 0.67 us
  other arithmetic: 4.72 us -> 0 us
    pallas_call x0 -> x2, Pallas kernels: none -> 73.6 us  [the longest x1 65.3 us: fast_body(): pl.pallas_call(functools.partial(exchange_kernel, n_fsdp), out_shape=(jax...]
    all_gather x3 -> x0, waiting for transfers between devices: 50.2 us -> none  [the longest x2 27.1 us: body(): lax.all_gather(own_rows[inner_step], 'fsdp', axis=0, tiled=True)]
    unnamed x5 -> x0, waiting for transfers between devices: 47 us -> none
    psum x1 -> x0, blocking collectives: 39.8 us -> none  [body(): squares = lax.psum(jnp.sum(corrected * corrected), ('replica', 'fsdp'))]
    dot_general x2 -> x0, matrix products: 22.2 us -> none  [row_gradient(): return jnp.dot(scaled, portion, preferred_element_type=jnp.float32)]
    unnamed x11 -> x14, local copies, waits for them, and re-layouts: 15.3 us -> 5.38 us
    all_gather x1 -> x0, local copies, waits for them, and re-layouts: 9.1 us -> none  [body(): anchor_island = lax.all_gather(anchor, 'replica', axis=1, tiled=True)]
    sub x1 -> x0, other arithmetic: 3.59 us -> none  [body(): new_anchor = anchor - OUTER_RATE * (MOMENT_DECAY * new_momentum + clipped)]
  transfers between devices with their start and end apart: 4 -> 0, of which waited for: 4 -> 0; matrix products, arithmetic and copies ran while one was open for 18% -> 0% of each run, Pallas kernels for 0% -> 0%
where the time goes in v1:
time: 79.9 us; the launch traced here: 79.6 us
  Pallas kernels  73.6 us (92%)
  local copies, waits for them, and re-layouts  5.38 us (7%)
    pallas_call x1, Pallas kernels, fast_body(): pl.pallas_call(functools.partial(exchange_kernel, n_fsdp), out_shape=(jax...  65.3 us
    pallas_call x1, Pallas kernels, fast_body(): pl.pallas_call(functools.partial(update_kernel, CLIP_SHARE * math.sqrt(D...  8.33 us
    unnamed x14, local copies, waits for them, and re-layouts  5.38 us

profile of v1, /device:TPU:0, one launch (start us, length us, event | category | flops | bytes accessed | tf_op | source)
XLA Modules:
  0.0 79.6 jit_solution(597932627940568167)
XLA Ops:
  0.6 0.0 copy-start
  0.6 1.4 %copy-done = f32[416,832]{1,0:T(8,128)S(1)} copy-done((f32[416,832]{1,0:T(8,128)S(1)}, f32[416,832]{1,0:T(8,128)}, u32[]{:S(2)}) %copy-start) | copy-done | bytes 1384472
  2.0 0.0 copy-start.2
  2.0 1.4 %copy-done.2 = f32[416,832]{1,0:T(8,128)S(1)} copy-done((f32[416,832]{1,0:T(8,128)S(1)}, f32[416,832]{1,0:T(8,128)}, u32[]{:S(2)}) %copy-start.2) | copy-done | bytes 1384472
  3.4 0.0 copy-start.4
  3.4 1.0 %copy-done.4 = bf16[1,2,416,256]{3,2,1,0:T(8,128)(2,1)S(1)} copy-done((bf16[1,2,416,256]{3,2,1,0:T(8,128)(2,1)S(1)}, bf16[1,2,416,256]{3,2,1,0:T(8,128)(2,1)}, u32[]{:S(2)}) %copy-start.4) | copy-done | bytes 426008
  4.4 0.0 copy-start.5
  4.4 0.9 %copy-done.5 = bf16[1,32,3328]{2,1,0:T(8,128)(2,1)S(1)} copy-done((bf16[1,32,3328]{2,1,0:T(8,128)(2,1)S(1)}, bf16[1,32,3328]{2,1,0:T(8,128)(2,1)}, u32[]{:S(2)}) %copy-start.5) | copy-done | bytes 213016
  5.3 0.0 copy-start.6
  5.3 0.7 copy-done.6
  6.0 0.0 copy-start.1
  6.0 0.0 copy-start.3
  6.0 65.3 %exchange.1 = (bf16[4,416,832]{2,1,0:T(8,128)(2,1)}, bf16[4,512,832]{2,1,0:T(8,128)(2,1)}, f32[416,832]{1,0:T(8,128)S(1)}, bf16[416,512]{1,0:T(8,128)(2,1)S(1)}, f32[8,128]{1,0:T(8,128)S(1)}) custom-call(s32[1,2,32]{2,1,0:T(2,128)S(1)} %copy-done.6, bf16[1,416,3328]{2,1,0:T(8,128)(2,1)} %prev_ref.1, f32[416,832]{1,0:T(8,128)S(1)} %copy-done, ...), custom_call_target="tpu_custom_call" | custom-call | tf_op jit(solution)/shard_map/exchange/pallas_call | solution.py:356
  71.3 0.0 copy-done.1
  71.3 0.0 copy-done.3
  71.3 8.3 %update.1 = (bf16[1,416,3328]{2,1,0:T(8,128)(2,1)}, f32[416,832]{1,0:T(8,128)}, f32[416,832]{1,0:T(8,128)}) custom-call(bf16[4,416,832]{2,1,0:T(8,128)(2,1)} %get-tuple-element.8.ag_ref, bf16[4,512,832]{2,1,0:T(8,128)(2,1)} %get-tuple-element.9.bb_ref, bf16[416,512]{1,0:T(8,128)(2,1)S(1)} %get-tuple-element.10.scaled_ref, ...), custom_call_target="tpu_custom_call" | custom-call | tf_op jit(solution)/shard_map/update/pallas_call | solution.py:402
Async XLA Ops:
  0.6 1.4 %copy-start = (f32[416,832]{1,0:T(8,128)S(1)}, f32[416,832]{1,0:T(8,128)}, u32[]{:S(2)}) copy-start(f32[416,832]{1,0:T(8,128)} %anchor_ref.3) | copy-start | bytes 4153348
  2.0 1.4 %copy-start.2 = (f32[416,832]{1,0:T(8,128)S(1)}, f32[416,832]{1,0:T(8,128)}, u32[]{:S(2)}) copy-start(f32[416,832]{1,0:T(8,128)} %mom_ref.3) | copy-start | bytes 4153348
  3.4 1.0 %copy-start.4 = (bf16[1,2,416,256]{3,2,1,0:T(8,128)(2,1)S(1)}, bf16[1,2,416,256]{3,2,1,0:T(8,128)(2,1)}, u32[]{:S(2)}) copy-start(bf16[1,2,416,256]{3,2,1,0:T(8,128)(2,1)} %cot_ref.1) | copy-start | bytes 1277956
  4.4 0.9 %copy-start.5 = (bf16[1,32,3328]{2,1,0:T(8,128)(2,1)S(1)}, bf16[1,32,3328]{2,1,0:T(8,128)(2,1)}, u32[]{:S(2)}) copy-start(bf16[1,32,3328]{2,1,0:T(8,128)(2,1)} %pool_ref.1) | copy-start | bytes 638980
  5.3 0.7 copy-start.6
  6.0 65.3 %copy-start.1 = (f32[416,832]{1,0:T(8,128)S(1)}, f32[416,832]{1,0:T(8,128)}, u32[]{:S(2)}) copy-start(f32[416,832]{1,0:T(8,128)} %anchor_ref.3) | copy-start | bytes 4153348
  6.0 65.3 %copy-start.3 = (f32[416,832]{1,0:T(8,128)S(1)}, f32[416,832]{1,0:T(8,128)}, u32[]{:S(2)}) copy-start(f32[416,832]{1,0:T(8,128)} %mom_ref.3) | copy-start | bytes 4153348

commit v2 on v1

--- a/solution.py
+++ b/solution.py
@@ -84,9 +84,9 @@
 
 
 def exchange_kernel(
-    n_fsdp,
+    n_fsdp, max_norm,
     ids_ref, prev_ref, anchor_ref, mom_ref, pool_ref, cot_ref,
-    ag_out, bb_out, corr_out, scaled_out, sq_out,
+    ag_out, pool_out, new_mom_out, new_anchor_out, coef_out,
     pv, blk, av, mv, plv, cv, ag, poolb, selb, bb, xr, yr, qs, s2, corr, preact, gram, sqv,
     local_sem, out_sem, send_sem, recv_sem, pool_send, pool_recv, sel_send, sel_recv,
 ):
@@ -225,7 +225,6 @@
         copy.start()
         outs.append(copy)
 
-    put(corr, corr_out, 0)
     put(ag.at[r], ag_out.at[r], 1)
 
     sq_x = send(sqv.at[0], sqv.at[4], 12, x_dev)
@@ -243,7 +242,7 @@
                 choice, block, preferred_element_type=jnp.float32
             ).astype(jnp.bfloat16)
 
-    put(bb, bb_out, 2)
+    put(poolb, pool_out, 2)
 
     sq_x.wait_recv()
     sqv[1] = sqv[0] + sqv[4]
@@ -283,7 +282,18 @@
     for k, copy in zip(hops, sq_z):
         copy.wait_recv()
         whole = whole + sqv[6 + k]
-    sq_out[...] = whole
+    factor = jnp.minimum(1.0, max_norm / jnp.sqrt(whole[0:1, 0:1] + 1e-06))
+
+    @pl.loop(0, 2)
+    def _(h):
+        part = pl.ds(pl.multiple_of(h * half, half), half)
+        clipped = factor * corr[part, :]
+        new_mom = MOMENT_DECAY * mv[part, :] + clipped
+        mv[part, :] = new_mom
+        av[part, :] = av[part, :] - OUTER_RATE * (MOMENT_DECAY * new_mom + clipped)
+
+    put(mv, new_mom_out, 0)
+    put(av, new_anchor_out, 6)
 
     in_cot.wait()
     gram_high = gram[...].astype(jnp.bfloat16)
@@ -299,14 +309,18 @@
         part = pl.ds(pl.multiple_of(h * half, half), half)
         first = preact[part, pl.ds(0, n_tok)] / root_width
         scaled = (cv[0, part, :].astype(jnp.float32) * silu_slope(first)).astype(jnp.bfloat16)
-        scaled_out[part, pl.ds(0, n_tok)] = scaled
         moved = jnp.dot(scaled, gram_high, preferred_element_type=jnp.float32)
         moved = moved + jnp.dot(scaled, gram_low, preferred_element_type=jnp.float32)
         second = (1.0 - INNER_DECAY) * preact[part, pl.ds(n_tok, n_tok)]
         second = (second - INNER_RATE * (moved / root_width)) / root_width
-        scaled_out[part, pl.ds(n_tok, n_tok)] = (
-            cv[1, part, :].astype(jnp.float32) * silu_slope(second)
-        ).astype(jnp.bfloat16)
+        later = (cv[1, part, :].astype(jnp.float32) * silu_slope(second)).astype(jnp.bfloat16)
+        coef = (1.0 - INNER_DECAY) * jnp.dot(
+            scaled, selb[:, 0, :, :].reshape(n_tok, n_tok), preferred_element_type=jnp.float32
+        )
+        coef = coef + jnp.dot(
+            later, selb[:, 1, :, :].reshape(n_tok, n_tok), preferred_element_type=jnp.float32
+        )
+        coef_out[part, :] = ((INNER_RATE / root_width) * coef).astype(jnp.bfloat16)
 
     for copy in started:
         copy.wait_send()
@@ -317,28 +331,18 @@
 
 
 def update_kernel(
-    max_norm, root_width,
-    ag_ref, bb_ref, scaled_ref, sq_ref, corr_ref, mom_ref, anchor_ref,
+    ag_ref, pool_ref, coef_ref, mom_ref, anchor_ref,
     delta_ref, new_anchor_ref, new_mom_ref,
 ):
     width = ag_ref.shape[2]
-    n_tok = bb_ref.shape[1] // 2
     keep = 1.0 - INNER_DECAY
     for b in range(2):
-        first = jnp.dot(
-            scaled_ref[:, :n_tok], bb_ref[b, :n_tok, :], preferred_element_type=jnp.float32
-        )
-        second = jnp.dot(
-            scaled_ref[:, n_tok:], bb_ref[b, n_tok:, :], preferred_element_type=jnp.float32
-        )
-        moved = (INNER_RATE * keep / root_width) * first + (INNER_RATE / root_width) * second
+        rows = pool_ref[:, b, :, :].reshape(coef_ref.shape[1], width)
+        moved = jnp.dot(coef_ref[...], rows, preferred_element_type=jnp.float32)
         value = (1.0 - keep * keep) * ag_ref[b].astype(jnp.float32) + moved
         delta_ref[0, :, width * b : width * (b + 1)] = value.astype(jnp.bfloat16)
-    factor = jnp.minimum(1.0, max_norm / jnp.sqrt(sq_ref[0:1, 0:1] + 1e-06))
-    clipped = factor * corr_ref[...]
-    new_mom = MOMENT_DECAY * mom_ref[...] + clipped
-    new_mom_ref[...] = new_mom
-    new_anchor_ref[...] = anchor_ref[...] - OUTER_RATE * (MOMENT_DECAY * new_mom + clipped)
+    new_mom_ref[...] = mom_ref[...]
+    new_anchor_ref[...] = anchor_ref[...]
 
 
 def fast_body(anchor, prev_delta, momentum, pool, ids, cotangent):
@@ -350,20 +354,20 @@
     half = rows // 2
     n_line = n_fsdp // 2
     bf16, f32 = jnp.bfloat16, jnp.float32
-    any_spec = pl.BlockSpec(memory_space=pl.ANY)
+    hbm_spec = pl.BlockSpec(memory_space=pltpu.HBM)
     vmem_spec = pl.BlockSpec(memory_space=pltpu.VMEM)
     dma = pltpu.SemaphoreType.DMA
-    ag, bb, corr, scaled, sq = pl.pallas_call(
-        functools.partial(exchange_kernel, n_fsdp),
+    ag, rows_all, moved_mom, moved_anchor, coef = pl.pallas_call(
+        functools.partial(exchange_kernel, n_fsdp, CLIP_SHARE * math.sqrt(D * HW)),
         out_shape=(
             jax.ShapeDtypeStruct((4, rows, width), bf16),
-            jax.ShapeDtypeStruct((4, 2 * n_tok, width), bf16),
+            jax.ShapeDtypeStruct((n_fsdp, 4, tok, width), bf16),
             jax.ShapeDtypeStruct((rows, width), f32),
-            jax.ShapeDtypeStruct((rows, 2 * n_tok), bf16),
-            jax.ShapeDtypeStruct((8, 128), f32),
+            jax.ShapeDtypeStruct((rows, width), f32),
+            jax.ShapeDtypeStruct((rows, n_tok), bf16),
         ),
-        in_specs=[vmem_spec] + [any_spec] * 5,
-        out_specs=(any_spec, any_spec, any_spec, vmem_spec, vmem_spec),
+        in_specs=[vmem_spec] + [hbm_spec] * 5,
+        out_specs=(hbm_spec, hbm_spec, hbm_spec, hbm_spec, vmem_spec),
         scratch_shapes=[
             pltpu.VMEM((rows, full), bf16),
             pltpu.VMEM((4, rows, width), bf16),
@@ -384,7 +388,7 @@
             pltpu.VMEM((n_tok, n_tok), f32),
             pltpu.VMEM((6 + n_line, 8, 128), f32),
             dma((6,)),
-            dma((6,)),
+            dma((7,)),
             dma((14 + n_line,)),
             dma((14 + n_line,)),
             dma((2 * n_line,)),
@@ -393,14 +397,14 @@
             dma((2 * n_line,)),
         ],
         compiler_params=pltpu.CompilerParams(
-            collective_id=0, has_side_effects=True, vmem_limit_bytes=48 * 1024 * 1024
+            collective_id=0, has_side_effects=True, vmem_limit_bytes=63 * 1024 * 1024
         ),
         name="exchange",
     )(ids, prev_delta, anchor, momentum, pool, cotangent)
     quarter = rows // 4
     by_rows = pl.BlockSpec((quarter, width), lambda c, i: (2 * c + i, 0))
     delta, new_anchor, new_momentum = pl.pallas_call(
-        functools.partial(update_kernel, CLIP_SHARE * math.sqrt(D * HW), math.sqrt(D)),
+        update_kernel,
         grid=(2, 2),
         out_shape=(
             jax.ShapeDtypeStruct(prev_delta.shape, bf16),
@@ -409,10 +413,8 @@
         ),
         in_specs=[
             pl.BlockSpec((2, half, width), lambda c, i: (c, i, 0)),
-            pl.BlockSpec((2, 2 * n_tok, width), lambda c, i: (c, 0, 0)),
-            pl.BlockSpec((half, 2 * n_tok), lambda c, i: (i, 0)),
-            pl.BlockSpec((8, 128), lambda c, i: (0, 0)),
-            by_rows,
+            pl.BlockSpec((n_fsdp, 2, tok, width), lambda c, i: (0, c, 0, 0)),
+            pl.BlockSpec((half, n_tok), lambda c, i: (i, 0)),
             by_rows,
             by_rows,
         ],
@@ -421,9 +423,9 @@
             by_rows,
             by_rows,
         ),
-        compiler_params=pltpu.CompilerParams(vmem_limit_bytes=48 * 1024 * 1024),
+        compiler_params=pltpu.CompilerParams(vmem_limit_bytes=63 * 1024 * 1024),
         name="update",
-    )(ag, bb, scaled, sq, corr, momentum, anchor)
+    )(ag, rows_all, coef, moved_mom, moved_anchor)
     return (delta, new_anchor, new_momentum)
 
 

time: 79.9 us -> 75.1 us (0.940)
  local copies, waits for them, and re-layouts: 5.38 us -> 0 us
    unnamed x14 -> x0, local copies, waits for them, and re-layouts: 5.38 us -> none
where the time goes in v2:
time: 75.1 us; the launch traced here: 75 us
  Pallas kernels  74.3 us (99%)
    pallas_call x1, Pallas kernels, fast_body(): pl.pallas_call(functools.partial(exchange_kernel, n_fsdp, CLIP_SHARE * ma...  67.5 us
    pallas_call x1, Pallas kernels, fast_body(): pl.pallas_call(update_kernel, grid=(2, 2), out_shape=(jax.ShapeDtypeStruc...  6.86 us

profile of v2, /device:TPU:0, one launch (start us, length us, event | category | flops | bytes accessed | tf_op | source)
XLA Modules:
  0.0 75.0 jit_solution(18070963698183951461)
XLA Ops:
  0.6 67.5 %exchange.1 = (bf16[4,416,832]{2,1,0:T(8,128)(2,1)}, bf16[8,4,32,832]{3,2,1,0:T(8,128)(2,1)}, f32[416,832]{1,0:T(8,128)}, f32[416,832]{1,0:T(8,128)}, bf16[416,256]{1,0:T(8,128)(2,1)}) custom-call(s32[1,2,32]{2,1,0:T(2,128)} %ids_ref.1, bf16[1,416,3328]{2,1,0:T(8,128)(2,1)} %prev_ref.1, f32[416,832]{1,0:T(8,128)} %anchor_ref.1, f32[416,832]{1,0:T(8,128)} %mom_ref.1, ...), custom_call_target="tpu_custom_call" | custom-call | tf_op jit(solution)/shard_map/exchange/pallas_call | solution.py:360
  68.1 6.9 %update.1 = (bf16[1,416,3328]{2,1,0:T(8,128)(2,1)}, f32[416,832]{1,0:T(8,128)}, f32[416,832]{1,0:T(8,128)}) custom-call(bf16[4,416,832]{2,1,0:T(8,128)(2,1)} %get-tuple-element.8.ag_ref, bf16[8,4,32,832]{3,2,1,0:T(8,128)(2,1)} %get-tuple-element.9.pool_ref, bf16[416,256]{1,0:T(8,128)(2,1)} %get-tuple-element.10.coef_ref, ...), custom_call_target="tpu_custom_call" | custom-call | tf_op jit(solution)/shard_map/update/pallas_call | solution.py:406
